TPU v7x, 256 devices: a whole 4x4x8 slice. The times are simulated.
256 devices in a mesh: pop: 16 (over y_hi, z), tp: 16 (over x, y_lo, core).
Axes of the slice: x: 4, y: 4 (y_hi: 2, y_lo: 2; y = y_hi * 2 + y_lo), z: 8, core: 2. Of those that a mesh axis runs over, the one named last changes fastest.
Arguments:
- tokens: bfloat16 [4096, 5120], P('pop'), may hold values from -6 to 6
- gate_weight: bfloat16 [5120, 14336], P('pop', 'tp'), may hold values from -0.078125 to 0.078125
- up_weight: bfloat16 [5120, 14336], P('pop', 'tp'), may hold values from -0.078125 to 0.078125
- down_weight: bfloat16 [5120, 14336], P('pop', 'tp'), may hold values from -0.0625 to 0.0625
- switch_velocity: float32 [5120, 14336], P('pop', 'tp'), may hold values from -6 to 6
- up_moment: float32 [5120, 14336], P('pop', 'tp'), may hold values from -6 to 6
- down_moment: float32 [5120, 14336], P('pop', 'tp'), may hold values from -6 to 6
- gate_in: bfloat16 [16, 5120], P('pop'), may hold values from -6 to 6
- switch_target_scaling: bfloat16 [16, 14336], P('pop', 'tp'), may hold values from -6 to 6
- up_in: bfloat16 [16, 5120], P('pop'), may hold values from -6 to 6
- up_output_factor: bfloat16 [16, 14336], P('pop', 'tp'), may hold values from -6 to 6
- down_in: bfloat16 [16, 14336], P('pop', 'tp'), may hold values from -6 to 6
- down_out: bfloat16 [16, 5120], P('pop'), may hold values from -6 to 6
- ranks: int32 [16], replicated, may hold values from 0 to 15, each once
- slot_member: int32 [16], replicated, may hold values from 0 to 15, each once
Outputs:
- evaluation: bfloat16 [16, 256, 5120], P('pop', None, 'tp')
- new_gate_moment: float32 [5120, 14336], P('pop', 'tp')
- new_up_moment: float32 [5120, 14336], P('pop', 'tp')
- new_down_moment: float32 [5120, 14336], P('pop', 'tp')
Inputs may be any that keep to these rules, and one draw needn't show every extreme that they name: `ranks`: each member has one rank, each of 0 to 15 once. `slot_member`: each member is evaluated in exactly one slot.
All inputs are finite; a program needn't handle non-finite values.
Results may differ from a plain program's by a relative error of at most 0.028.
Values may be sent and summed in bfloat16 or wider, within the bound.
No kernel may reach another device: no remote copies, remote signals or barrier semaphores. Data moves between devices by JAX's collectives and lax.ppermute only.
A program may use at most 128 MiB of HBM per device.

v0:
```python
import functools
import math

import jax
import jax.numpy as jnp
from jax import lax
from jax.experimental import pallas as pl
from jax.experimental.pallas import tpu as pltpu
from jax.sharding import Mesh
from jax.sharding import PartitionSpec as P

SIGMA = 0.005
BETA = 0.9
F32 = jnp.float32
BF16 = jnp.bfloat16
NZ = 8
NX = 4
SPARE = 48
LIMIT = 62 * 1024 * 1024

UP = [(i, (i + 1) % NZ) for i in range(NZ)]
DOWN = [(i, (i - 1) % NZ) for i in range(NZ)]
SWAP = [(0, 1), (1, 0)]


def at(array, index):
    starts = (index,) + (0,) * (array.ndim - 1)
    sizes = (1,) + array.shape[1:]
    return lax.dynamic_slice(array, starts, sizes, allow_negative_indices=False)[0]


def window(array, start, size, axis):
    starts = [0] * array.ndim
    starts[axis] = start
    sizes = list(array.shape)
    sizes[axis] = size
    return lax.dynamic_slice(array, starts, sizes, allow_negative_indices=False)


def behind(array, *others):
    return lax.optimization_barrier((array, *others))[0]


def ring(block, after=None):
    if after is not None:
        block = behind(block, *after)
    half = block.shape[0] // 2
    got = [block] + [None] * (NZ - 1)
    fore = back = block
    for k in range(1, NZ // 2):
        fore = lax.ppermute(fore, "z", UP)
        back = lax.ppermute(back, "z", DOWN)
        got[k], got[NZ - k] = fore, back
    got[NZ // 2] = (lax.ppermute(fore[:half], "z", UP), lax.ppermute(back[half:], "z", DOWN))
    return got


def base_kernel(count, depth, where, *refs):
    pieces, blocks = refs[:count], refs[count : 2 * count]
    out = refs[-1]
    total = refs[2 * count][...] if len(refs) > 2 * count + 1 else None
    for piece, block in zip(pieces, blocks):
        term = jnp.dot(piece[0], block[:depth, :], preferred_element_type=F32)
        total = term if total is None else total + term
    out[...] = total


def base_sum(where, pieces, steps, blocks, total=None):
    _, rows, depth = pieces.shape
    cols = blocks[0].shape[1]
    count = len(steps)
    half = rows // 2
    extra = [] if total is None else [total]
    wide = pl.BlockSpec((half, cols), lambda i, s: (i, 0))

    def place(k):
        return pl.BlockSpec((1, half, depth), lambda i, s: ((s[0] - k) & (NZ - 1), i, 0))

    return pl.pallas_call(
        functools.partial(base_kernel, count, depth),
        grid_spec=pltpu.PrefetchScalarGridSpec(
            num_scalar_prefetch=1,
            grid=(2,),
            in_specs=[place(k) for k in steps]
            + [pl.BlockSpec(block.shape, lambda i, s: (0, 0)) for block in blocks]
            + [wide] * len(extra),
            out_specs=wide,
        ),
        out_shape=jax.ShapeDtypeStruct((rows, cols), F32),
        compiler_params=pltpu.CompilerParams(vmem_limit_bytes=LIMIT),
        cost_estimate=pl.CostEstimate(
            flops=2 * rows * cols * depth * count,
            bytes_accessed=count * (rows + cols) * depth * 2 + 4 * rows * cols,
            transcendentals=0,
        ),
    )(where, *[pieces] * count, *blocks, *extra)


def part_kernel(where, hidden, across, tails, block, out):
    term = lax.dot_general(
        block[...], hidden[...], (((1,), (1,)), ((), ())), preferred_element_type=F32
    )
    size = hidden.shape[0] // 2
    for r in range(2):
        lanes = slice(r * size, (r + 1) * size)
        value = term[:, lanes] + tails[0, :, r : r + 1] * across[:, lanes]
        out[0, 0, :, lanes] = value.astype(BF16)


def part_products(where, hidden, across, tails, weight, n1):
    rows, cols = hidden.shape
    span = tails.shape[1]

    def block_of(i):
        return (i >> 1) * 4 + n1 * 2 + (i & 1)

    return pl.pallas_call(
        part_kernel,
        grid_spec=pltpu.PrefetchScalarGridSpec(
            num_scalar_prefetch=1,
            grid=(4,),
            in_specs=[
                pl.BlockSpec((rows, cols), lambda i, s: (0, 0)),
                pl.BlockSpec((1, rows), lambda i, s: (0, 0)),
                pl.BlockSpec((1, span, 2), lambda i, s: (block_of(i), 0, 0)),
                pl.BlockSpec((span, cols), lambda i, s: (block_of(i), 0)),
            ],
            out_specs=pl.BlockSpec(
                (1, 1, span, rows), lambda i, s: ((i & 1) ^ s[1], i >> 1, 0, 0)
            ),
        ),
        out_shape=jax.ShapeDtypeStruct((2, 2, span, rows), BF16),
        compiler_params=pltpu.CompilerParams(vmem_limit_bytes=LIMIT),
        cost_estimate=pl.CostEstimate(
            flops=2 * rows * cols * span * 4,
            bytes_accessed=2 * (rows * cols + 4 * span * (cols + rows)),
            transcendentals=0,
        ),
    )(where, hidden, across, tails, weight)


def body(
    tokens,
    gate_weight,
    up_weight,
    down_weight,
    switch_velocity,
    up_moment,
    down_moment,
    gate_in,
    switch_target_scaling,
    up_in,
    up_output_factor,
    down_in,
    down_out,
    ranks,
    slot_member,
):
    rows, width = tokens.shape
    span, cols = gate_weight.shape
    members = ranks.shape[0]
    yh, z, x, yl, c = (lax.axis_index(name) for name in ("yh", "z", "x", "yl", "c"))
    position = yh * NZ + z
    mask = NZ - 1
    half = width // 2

    outer = jnp.concatenate([switch_target_scaling, up_output_factor, down_in], axis=0)
    inner = jnp.concatenate([gate_in, up_in, down_out], axis=1).reshape(-1, 128)
    fill = -inner.shape[0] % (cols // 128)
    inner = jnp.concatenate([inner, jnp.zeros((fill, 128), BF16)], axis=0).reshape(-1, cols)
    depth = inner.shape[0]
    spare = jnp.zeros((SPARE // 2 - depth - 3, cols), BF16)
    mine = jnp.concatenate([inner, outer, spare], axis=0)
    both = jnp.concatenate([mine, lax.ppermute(mine, "yh", SWAP)], axis=0)
    up_block = jnp.concatenate([up_weight, both], axis=0)

    gates = ring(gate_weight)
    ups = ring(up_block)
    downs = lax.all_gather(behind(down_weight, gates[2]), "z", axis=0, tiled=True)

    where = jnp.stack([z, c])
    near = window(tokens, yh * half, half, 1)
    other = behind(window(tokens, (1 - yh) * half, half, 1), both)
    pair = jnp.concatenate([near, lax.ppermute(other, "yh", SWAP)], axis=0)
    blocks = pair.reshape(2 * rows, NZ, span).transpose(1, 0, 2)

    def base(found):
        early = (0, 1, 7, 2, 6)
        total = base_sum(
            behind(where, found[3], found[5]), blocks, early, [found[k] for k in early]
        )
        last = jnp.concatenate(found[4], axis=0)
        total = base_sum(where, blocks, (3, 5, 4), [found[3], found[5], last], total)
        sent = lax.ppermute(total[rows:].astype(BF16), "yh", SWAP)
        return total[:rows] + sent.astype(F32)

    base_gate = base(gates)
    base_up = base(ups)

    ups[4] = jnp.concatenate(ups[4], axis=0)
    found = jnp.stack([block[span:] for block in ups]).reshape(members, SPARE // 2, cols)
    outer = found[:, depth : depth + 3]

    def entry_of(member):
        return (((z - member) & mask) << 1) | ((member >> 3) ^ yh)

    own = entry_of(at(slot_member, position))
    partner = entry_of(at(slot_member, (1 - yh) * NZ + z))

    inner = found[:, :depth].reshape(members, -1)[:, : 3 * width].reshape(members, 3, width)
    own_inner, own_outer = at(inner, own), at(outer, own)
    shifts = SIGMA * lax.dot_general(
        tokens, own_inner[:2], (((1,), (1,)), ((), ())), preferred_element_type=F32
    )
    gate = base_gate + shifts[:, 0:1] * own_outer[0].astype(F32)[None, :]
    upper = base_up + shifts[:, 1:2] * own_outer[1].astype(F32)[None, :]
    hidden = (jax.nn.silu(gate) * upper).astype(BF16)
    guests = lax.ppermute(hidden, "yh", SWAP)
    hiddens = jnp.concatenate([hidden, guests], axis=0)
    across = [
        jnp.dot(hidden, own_outer[2], preferred_element_type=F32),
        jnp.dot(guests, at(outer, partner)[2], preferred_element_type=F32),
    ]
    across = SIGMA * jnp.concatenate(across).reshape(1, -1)
    tails = window(jnp.stack([own_inner[2], at(inner, partner)[2]]), yh * half, half, 1)
    tails = tails.astype(F32).reshape(2, NZ, span).transpose(1, 2, 0)

    quad = []
    for n1 in range(2):
        parts = part_products(where, hiddens, across, tails, downs, n1)
        pairs = parts[0].astype(F32) + lax.ppermute(parts[1], "c", SWAP).astype(F32)
        pairs = pairs.astype(BF16)

        def piece_for(spot):
            return window(at(pairs, spot & 1), ((spot >> 1) ^ yh) * rows, rows, 1)

        value = piece_for(x).astype(F32)
        for d in range(1, NX):
            value = value + lax.ppermute(
                piece_for((x + d) & (NX - 1)), "x", [(i, (i + d) % NX) for i in range(NX)]
            ).astype(F32)
        quad.append(value.astype(BF16))
    quad = jnp.stack(quad)

    def place(flip):
        perm = []
        for a in range(2):
            for b in range(NX):
                for e in range(2):
                    source = (a * NX + b) * 2 + e
                    target = ((b // 2) * NX + (a * 2 + b % 2)) * 2 + (e ^ flip)
                    perm.append((source, target))
        return lax.ppermute(at(quad, yl ^ flip), ("yh", "x", "yl"), perm).astype(F32)

    evaluation = (place(0) + place(1)).astype(BF16).T[None]

    coef = (ranks.astype(F32) / (members - 1) - 0.5) / math.sqrt(members)
    entries = jnp.arange(members, dtype=jnp.int32)
    coef = coef[((yh ^ (entries & 1)) << 3) | ((z - (entries >> 1)) & mask)]
    spans = window(inner, position * span, span, 2)

    def moment(old, left, right):
        weighted = coef[:, None] * left.astype(F32)
        return BETA * old + jnp.dot(
            weighted.T, right.astype(F32), precision=lax.Precision.HIGHEST
        )

    new_gate = moment(switch_velocity, spans[:, 0], outer[:, 0])
    new_up = moment(up_moment, spans[:, 1], outer[:, 1])
    new_down = moment(down_moment, spans[:, 2], outer[:, 2])
    return (evaluation, new_gate, new_up, new_down)


def solution(mesh):
    fine = Mesh(mesh.devices.reshape(2, NZ, NX, 2, 2), ("yh", "z", "x", "yl", "c"))
    pop, tp = ("yh", "z"), ("x", "yl", "c")
    line, grid = P(pop, None), P(pop, tp)
    placed = (line,) + (grid,) * 6 + (line, grid, line, grid, grid, line, P(), P())
    return jax.shard_map(
        body,
        mesh=fine,
        in_specs=placed,
        out_specs=(P(pop, None, tp), grid, grid, grid),
        check_vma=False,
    )
```

profile of v0, /device:TPU:6, one launch (start us, length us, event | category | flops | bytes accessed | tf_op | source)
XLA Modules:
  0.0 297.2 jit_solution(6197203517799965348)
XLA Ops:
  9.2 17.1 %collective-permute-done.2.refs_6_ = bf16[320,896]{1,0:T(8,128)(2,1)S(1)} collective-permute-done((bf16[320,896]{1,0:T(8,128)(2,1)}, bf16[320,896]{1,0:T(8,128)(2,1)S(1)}, u32[]{:S(2)}, u32[]{:S(2)}) %collective-permute-start.2) | collective-permute-done | bytes 573472 | tf_op jit(solution)/shard_map/ppermute | solution.py:51
  27.2 15.5 %collective-permute-done.3.refs_8_ = bf16[320,896]{1,0:T(8,128)(2,1)} collective-permute-done((bf16[320,896]{1,0:T(8,128)(2,1)S(1)}, bf16[320,896]{1,0:T(8,128)(2,1)}, u32[]{:S(2)}, u32[]{:S(2)}) %collective-permute-start.3) | collective-permute-done | bytes 573472 | tf_op jit(solution)/shard_map/ppermute | solution.py:51
  44.5 3.3 %collective-permute-start = (bf16[24,896]{1,0:T(8,128)(2,1)S(1)}, bf16[24,896]{1,0:T(8,128)(2,1)S(1)}, u32[]{:S(2)}, u32[]{:S(2)}) collective-permute-start(bf16[24,896]{1,0:T(8,128)(2,1)S(1)} %concatenate.45), channel_id=1, source_target_pairs={{0,128},{128,0},{1,129},{129,1},{2,130},{130,2},{3,131},{131,3},{4... | collective-permute-start | bytes 129032 | tf_op jit(solution)/shard_map/ppermute | solution.py:174
  58.0 3.3 %collective-permute-start.1 = (bf16[256,2560]{0,1:T(8,128)(2,1)}, bf16[256,2560]{0,1:T(8,128)(2,1)}, u32[]{:S(2)}, u32[]{:S(2)}) collective-permute-start(bf16[256,2560]{0,1:T(8,128)(2,1)} %copy.30), channel_id=1, source_target_pairs={{0,128},{128,0},{1,129},{129,1},{2,130},{130,2},{3,131},{131,3},{4... | collective-permute-start | bytes 3932168 | tf_op jit(solution)/shard_map/ppermute | solution.py:184
  61.2 10.9 %collective-permute-done.5.refs_7_ = bf16[320,896]{1,0:T(8,128)(2,1)} collective-permute-done((bf16[320,896]{1,0:T(8,128)(2,1)}, bf16[320,896]{1,0:T(8,128)(2,1)}, u32[]{:S(2)}, u32[]{:S(2)}) %collective-permute-start.5) | collective-permute-done | bytes 573472 | tf_op jit(solution)/shard_map/ppermute | solution.py:52
  78.0 3.5 %collective-permute-done.11.refs_6_ = bf16[368,896]{1,0:T(8,128)(2,1)} collective-permute-done((bf16[368,896]{1,0:T(8,128)(2,1)S(1)}, bf16[368,896]{1,0:T(8,128)(2,1)}, u32[]{:S(2)}, u32[]{:S(2)}) %collective-permute-start.11) | collective-permute-done | bytes 659488 | tf_op jit(solution)/shard_map/ppermute | solution.py:51
  81.5 18.9 %collective-permute-done.14.refs_7_ = bf16[368,896]{1,0:T(8,128)(2,1)} collective-permute-done((bf16[368,896]{1,0:T(8,128)(2,1)S(1)}, bf16[368,896]{1,0:T(8,128)(2,1)}, u32[]{:S(2)}, u32[]{:S(2)}) %collective-permute-start.14) | collective-permute-done | bytes 659488 | tf_op jit(solution)/shard_map/ppermute | solution.py:52
  104.4 20.6 %collective-permute-done.6.refs_9_ = bf16[320,896]{1,0:T(8,128)(2,1)} collective-permute-done((bf16[320,896]{1,0:T(8,128)(2,1)}, bf16[320,896]{1,0:T(8,128)(2,1)}, u32[]{:S(2)}, u32[]{:S(2)}) %collective-permute-start.6) | collective-permute-done | bytes 573472 | tf_op jit(solution)/shard_map/ppermute | solution.py:52
  128.5 19.0 %collective-permute-done.15.refs_9_ = bf16[368,896]{1,0:T(8,128)(2,1)} collective-permute-done((bf16[368,896]{1,0:T(8,128)(2,1)}, bf16[368,896]{1,0:T(8,128)(2,1)}, u32[]{:S(2)}, u32[]{:S(2)}) %collective-permute-start.15) | collective-permute-done | bytes 659488 | tf_op jit(solution)/shard_map/ppermute | solution.py:52
  155.4 4.5 %collective-permute-done.7.refs_4_ = bf16[320,896]{1,0:T(8,128)(2,1)} collective-permute-done((bf16[320,896]{1,0:T(8,128)(2,1)}, bf16[320,896]{1,0:T(8,128)(2,1)}, u32[]{:S(2)}, u32[]{:S(2)}) %collective-permute-start.7) | collective-permute-done | bytes 573472 | tf_op jit(solution)/shard_map/ppermute | solution.py:52
  164.5 6.9 %shard_map.174.refs_6_ = f32[512,896]{1,0:T(8,128)} custom-call(s32[2]{0:T(128)} %pad_add_fusion.where, bf16[8,512,320]{2,1,0:T(8,128)(2,1)} %bitcast.130, bf16[8,512,320]{2,1,0:T(8,128)(2,1)} %bitcast.131, bf16[8,512,320]{2,1,0:T(8,128)(2,1)} %bitcast.132, bf16[8,512,320]{2,1,0:T(8,128)(2,1)} %bitcast.133, bf16[8,512,320]{2,1,0:T(8,128)(2,1)} %bitcast.134, ...), custom_call_target="tpu_custom_call" | custom-call | flops 1468006400 | bytes 6340608 | tf_op jit(solution)/shard_map/pallas_call | solution.py:79
  171.4 5.7 %collective-permute-done.9 = bf16[160,896]{1,0:T(8,128)(2,1)S(1)} collective-permute-done((bf16[160,896]{1,0:T(8,128)(2,1)}, bf16[160,896]{1,0:T(8,128)(2,1)S(1)}, u32[]{:S(2)}, u32[]{:S(2)}) %collective-permute-start.9) | collective-permute-done | bytes 286752 | tf_op jit(solution)/shard_map/ppermute | solution.py:54
  177.9 5.6 %shard_map.175 = f32[512,896]{1,0:T(8,128)} custom-call(s32[2]{0:T(128)} %pad_add_fusion.where, bf16[8,512,320]{2,1,0:T(8,128)(2,1)} %bitcast.135, bf16[8,512,320]{2,1,0:T(8,128)(2,1)} %bitcast.136, bf16[8,512,320]{2,1,0:T(8,128)(2,1)} %bitcast.137, bf16[320,896]{1,0:T(8,128)(2,1)} %collective-permute-done.4.refs_3_, ...), custom_call_target="tpu_custom_call" | custom-call | flops 880803840 | bytes 4538368 | tf_op jit(solution)/shard_map/pallas_call | solution.py:79
  190.5 7.0 %shard_map.176.refs_6_ = f32[512,896]{1,0:T(8,128)} custom-call(s32[2]{0:T(128)} %pad_add_fusion.where, bf16[8,512,320]{2,1,0:T(8,128)(2,1)} %bitcast.138, bf16[8,512,320]{2,1,0:T(8,128)(2,1)} %bitcast.139, bf16[8,512,320]{2,1,0:T(8,128)(2,1)} %bitcast.140, bf16[8,512,320]{2,1,0:T(8,128)(2,1)} %bitcast.141, bf16[8,512,320]{2,1,0:T(8,128)(2,1)} %bitcast.142, ...), custom_call_target="tpu_custom_call" | custom-call | flops 1468006400 | bytes 6340608 | tf_op jit(solution)/shard_map/pallas_call | solution.py:79
  204.0 5.6 %shard_map.177 = f32[512,896]{1,0:T(8,128)} custom-call(s32[2]{0:T(128)} %pad_add_fusion.where, bf16[8,512,320]{2,1,0:T(8,128)(2,1)} %bitcast.143, bf16[8,512,320]{2,1,0:T(8,128)(2,1)} %bitcast.144, bf16[8,512,320]{2,1,0:T(8,128)(2,1)} %bitcast.145, bf16[368,896]{1,0:T(8,128)(2,1)} %copy-done.4, bf16[368,896]{1,0:T(8,128)(2,1)} %collective-permute-done.16.refs_4_, ...), custom_call_target="tpu_custom_call" | custom-call | flops 880803840 | bytes 4538368 | tf_op jit(solution)/shard_map/pallas_call | solution.py:79
  224.3 3.4 %collective-permute-start.20 = (bf16[256,896]{1,0:T(8,128)(2,1)S(1)}, bf16[256,896]{1,0:T(8,128)(2,1)S(1)}, u32[]{:S(2)}, u32[]{:S(2)}) collective-permute-start(bf16[256,896]{1,0:T(8,128)(2,1)S(1)} %fusion.5), channel_id=1, source_target_pairs={{0,128},{128,0},{1,129},{129,1},{2,130},{130,2},{3,131},{131,3},{4... | collective-permute-start | bytes 1376264 | tf_op jit(solution)/shard_map/ppermute | solution.py:218
  228.1 6.5 %collective-permute-done.20 = bf16[256,896]{1,0:T(8,128)(2,1)S(1)} collective-permute-done((bf16[256,896]{1,0:T(8,128)(2,1)S(1)}, bf16[256,896]{1,0:T(8,128)(2,1)S(1)}, u32[]{:S(2)}, u32[]{:S(2)}) %collective-permute-start.20) | collective-permute-done | bytes 458784 | tf_op jit(solution)/shard_map/ppermute | solution.py:218
  236.4 5.9 %shard_map.179 = bf16[2,2,320,512]{3,2,1,0:T(8,128)(2,1)} custom-call(s32[2]{0:T(128)} %pad_add_fusion.where, bf16[512,896]{1,0:T(8,128)(2,1)} %pad_maximum_fusion.1.hidden, f32[1,512]{1,0:T(1,128)} %maximum_multiply_fusion.across, f32[8,320,2]{2,1,0:T(8,128)} %bitcast.146, bf16[2560,896]{1,0:T(8,128)(2,1)} %all-gather.2.cloned.1.call-done.block), custom_call_target="tpu_custom_call" | custom-call | flops 1174405120 | bytes 4521984 | tf_op jit(solution)/shard_map/pallas_call | solution.py:117
  245.5 5.8 %shard_map.178 = bf16[2,2,320,512]{3,2,1,0:T(8,128)(2,1)} custom-call(s32[2]{0:T(128)} %pad_add_fusion.where, bf16[512,896]{1,0:T(8,128)(2,1)} %pad_maximum_fusion.1.hidden, f32[1,512]{1,0:T(1,128)} %maximum_multiply_fusion.across, f32[8,320,2]{2,1,0:T(8,128)} %bitcast.147, bf16[2560,896]{1,0:T(8,128)(2,1)} %all-gather.2.cloned.1.call-done.block), custom_call_target="tpu_custom_call" | custom-call | flops 1174405120 | bytes 4521984 | tf_op jit(solution)/shard_map/pallas_call | solution.py:117
  258.5 3.3 %collective-permute-start.22 = (bf16[320,256]{1,0:T(8,128)(2,1)S(1)}, bf16[320,256]{1,0:T(8,128)(2,1)S(1)}, u32[]{:S(2)}, u32[]{:S(2)}) collective-permute-start(bf16[320,256]{1,0:T(8,128)(2,1)S(1)} %get-tuple-element.25), channel_id=1, source_target_pairs={{0,4},{4,8},{8,12},{12,0},{1,5},{5,9},{9,13},{13,1},{2,6},{6,10},{... | collective-permute-start | bytes 491528 | tf_op jit(solution)/shard_map/ppermute | solution.py:239
  262.2 3.7 %collective-permute-start.24 = (bf16[320,256]{1,0:T(8,128)(2,1)S(1)}, bf16[320,256]{1,0:T(8,128)(2,1)S(1)}, u32[]{:S(2)}, u32[]{:S(2)}) collective-permute-start(bf16[320,256]{1,0:T(8,128)(2,1)S(1)} %get-tuple-element.26), channel_id=1, source_target_pairs={{0,12},{4,0},{8,4},{12,8},{1,13},{5,1},{9,5},{13,9},{2,14},{6,2},{... | collective-permute-start | bytes 491528 | tf_op jit(solution)/shard_map/ppermute | solution.py:239
  265.9 4.0 %collective-permute-done.28 = bf16[320,256]{1,0:T(8,128)(2,1)S(1)} collective-permute-done((bf16[320,256]{1,0:T(8,128)(2,1)S(1)}, bf16[320,256]{1,0:T(8,128)(2,1)S(1)}, u32[]{:S(2)}, u32[]{:S(2)}) %collective-permute-start.28) | collective-permute-done | bytes 163872 | tf_op jit(solution)/shard_map/ppermute | solution.py:239
  274.0 6.2 %collective-permute-start.29 = (bf16[320,256]{1,0:T(8,128)(2,1)S(1)}, bf16[320,256]{1,0:T(8,128)(2,1)S(1)}, u32[]{:S(2)}, u32[]{:S(2)}) collective-permute-start(bf16[320,256]{1,0:T(8,128)(2,1)S(1)} %get-tuple-element.30), channel_id=1, source_target_pairs={{0,0},{2,2},{4,4},{6,6},{8,128},{10,130},{12,132},{14,134},{128,8}... | collective-permute-start | bytes 491528 | tf_op jit(solution)/shard_map/ppermute | solution.py:253
  286.0 3.6 %collective-permute-done.30 = bf16[320,256]{1,0:T(8,128)(2,1)S(1)} collective-permute-done((bf16[320,256]{1,0:T(8,128)(2,1)S(1)}, bf16[320,256]{1,0:T(8,128)(2,1)S(1)}, u32[]{:S(2)}, u32[]{:S(2)}) %collective-permute-start.30) | collective-permute-done | bytes 163872 | tf_op jit(solution)/shard_map/ppermute | solution.py:253
  (143 shorter events, 90.4 us)
Async XLA Ops:
  7.2 229.3 %all-gather.2.cloned.1.call-start = ((), (), s32[]{:S(2)}) async-start(), calls=%async_computation | async-start | bytes 5160960 | tf_op jit(solution)/shard_map/all_gather | solution.py:179
  7.2 19.1 %collective-permute-start.2 = (bf16[320,896]{1,0:T(8,128)(2,1)}, bf16[320,896]{1,0:T(8,128)(2,1)S(1)}, u32[]{:S(2)}, u32[]{:S(2)}) collective-permute-start(bf16[320,896]{1,0:T(8,128)(2,1)} %refs_5_.1), channel_id=1, source_target_pairs={{0,16},{16,32},{32,48},{48,64},{64,80},{80,96},{96,112},{112,0},{1... | collective-permute-start | bytes 1720328 | tf_op jit(solution)/shard_map/ppermute | solution.py:51
  27.2 15.5 %collective-permute-start.3 = (bf16[320,896]{1,0:T(8,128)(2,1)S(1)}, bf16[320,896]{1,0:T(8,128)(2,1)}, u32[]{:S(2)}, u32[]{:S(2)}) collective-permute-start(bf16[320,896]{1,0:T(8,128)(2,1)S(1)} %collective-permute-done.2.refs_6_), channel_id=1, source_target_pairs={{0,16},{16,32},{32,48},{48,64},{64,80},{80,96},{96,112},{112,0},{1... | collective-permute-start | bytes 1720328 | tf_op jit(solution)/shard_map/ppermute | solution.py:51
  47.7 24.4 %collective-permute-start.5 = (bf16[320,896]{1,0:T(8,128)(2,1)}, bf16[320,896]{1,0:T(8,128)(2,1)}, u32[]{:S(2)}, u32[]{:S(2)}) collective-permute-start(bf16[320,896]{1,0:T(8,128)(2,1)} %refs_5_.1), channel_id=1, source_target_pairs={{0,112},{16,0},{32,16},{48,32},{64,48},{80,64},{96,80},{112,96},{1... | collective-permute-start | bytes 1720328 | tf_op jit(solution)/shard_map/ppermute | solution.py:52
  51.1 30.4 %collective-permute-start.11 = (bf16[368,896]{1,0:T(8,128)(2,1)S(1)}, bf16[368,896]{1,0:T(8,128)(2,1)}, u32[]{:S(2)}, u32[]{:S(2)}) collective-permute-start(bf16[368,896]{1,0:T(8,128)(2,1)S(1)} %concatenate.49.refs_5_), channel_id=1, source_target_pairs={{0,16},{16,32},{32,48},{48,64},{64,80},{80,96},{96,112},{112,0},{1... | collective-permute-start | bytes 1978376 | tf_op jit(solution)/shard_map/ppermute | solution.py:51
  51.2 49.2 %collective-permute-start.14 = (bf16[368,896]{1,0:T(8,128)(2,1)S(1)}, bf16[368,896]{1,0:T(8,128)(2,1)}, u32[]{:S(2)}, u32[]{:S(2)}) collective-permute-start(bf16[368,896]{1,0:T(8,128)(2,1)S(1)} %concatenate.49.refs_5_), channel_id=1, source_target_pairs={{0,112},{16,0},{32,16},{48,32},{64,48},{80,64},{96,80},{112,96},{1... | collective-permute-start | bytes 1978376 | tf_op jit(solution)/shard_map/ppermute | solution.py:52
  58.0 91.0 %collective-permute-start.1 = (bf16[256,2560]{0,1:T(8,128)(2,1)}, bf16[256,2560]{0,1:T(8,128)(2,1)}, u32[]{:S(2)}, u32[]{:S(2)}) collective-permute-start(bf16[256,2560]{0,1:T(8,128)(2,1)} %copy.30), channel_id=1, source_target_pairs={{0,128},{128,0},{1,129},{129,1},{2,130},{130,2},{3,131},{131,3},{4... | collective-permute-start | bytes 3932168 | tf_op jit(solution)/shard_map/ppermute | solution.py:184
  72.1 52.8 %collective-permute-start.6 = (bf16[320,896]{1,0:T(8,128)(2,1)}, bf16[320,896]{1,0:T(8,128)(2,1)}, u32[]{:S(2)}, u32[]{:S(2)}) collective-permute-start(bf16[320,896]{1,0:T(8,128)(2,1)} %collective-permute-done.5.refs_7_), channel_id=1, source_target_pairs={{0,112},{16,0},{32,16},{48,32},{64,48},{80,64},{96,80},{112,96},{1... | collective-permute-start | bytes 1720328 | tf_op jit(solution)/shard_map/ppermute | solution.py:52
  81.5 46.2 %collective-permute-start.12 = (bf16[368,896]{1,0:T(8,128)(2,1)}, bf16[368,896]{1,0:T(8,128)(2,1)}, u32[]{:S(2)}, u32[]{:S(2)}) collective-permute-start(bf16[368,896]{1,0:T(8,128)(2,1)} %collective-permute-done.11.refs_6_), channel_id=1, source_target_pairs={{0,16},{16,32},{32,48},{48,64},{64,80},{80,96},{96,112},{112,0},{1... | collective-permute-start | bytes 1978376 | tf_op jit(solution)/shard_map/ppermute | solution.py:51
  100.4 47.2 %collective-permute-start.15 = (bf16[368,896]{1,0:T(8,128)(2,1)}, bf16[368,896]{1,0:T(8,128)(2,1)}, u32[]{:S(2)}, u32[]{:S(2)}) collective-permute-start(bf16[368,896]{1,0:T(8,128)(2,1)} %collective-permute-done.14.refs_7_), channel_id=1, source_target_pairs={{0,112},{16,0},{32,16},{48,32},{64,48},{80,64},{96,80},{112,96},{1... | collective-permute-start | bytes 1978376 | tf_op jit(solution)/shard_map/ppermute | solution.py:52
  103.5 50.2 %collective-permute-start.4 = (bf16[320,896]{1,0:T(8,128)(2,1)}, bf16[320,896]{1,0:T(8,128)(2,1)}, u32[]{:S(2)}, u32[]{:S(2)}) collective-permute-start(bf16[320,896]{1,0:T(8,128)(2,1)} %collective-permute-done.3.refs_8_), channel_id=1, source_target_pairs={{0,16},{16,32},{32,48},{48,64},{64,80},{80,96},{96,112},{112,0},{1... | collective-permute-start | bytes 1720328 | tf_op jit(solution)/shard_map/ppermute | solution.py:51
  125.0 34.9 %collective-permute-start.7 = (bf16[320,896]{1,0:T(8,128)(2,1)}, bf16[320,896]{1,0:T(8,128)(2,1)}, u32[]{:S(2)}, u32[]{:S(2)}) collective-permute-start(bf16[320,896]{1,0:T(8,128)(2,1)} %collective-permute-done.6.refs_9_), channel_id=1, source_target_pairs={{0,112},{16,0},{32,16},{48,32},{64,48},{80,64},{96,80},{112,96},{1... | collective-permute-start | bytes 1720328 | tf_op jit(solution)/shard_map/ppermute | solution.py:52
  127.7 61.5 %collective-permute-start.13 = (bf16[368,896]{1,0:T(8,128)(2,1)}, bf16[368,896]{1,0:T(8,128)(2,1)S(1)}, u32[]{:S(2)}, u32[]{:S(2)}) collective-permute-start(bf16[368,896]{1,0:T(8,128)(2,1)} %collective-permute-done.12.refs_8_), channel_id=1, source_target_pairs={{0,16},{16,32},{32,48},{48,64},{64,80},{80,96},{96,112},{112,0},{1... | collective-permute-start | bytes 1978376 | tf_op jit(solution)/shard_map/ppermute | solution.py:51
  147.5 38.4 %collective-permute-start.16 = (bf16[368,896]{1,0:T(8,128)(2,1)}, bf16[368,896]{1,0:T(8,128)(2,1)}, u32[]{:S(2)}, u32[]{:S(2)}) collective-permute-start(bf16[368,896]{1,0:T(8,128)(2,1)} %collective-permute-done.15.refs_9_), channel_id=1, source_target_pairs={{0,112},{16,0},{32,16},{48,32},{64,48},{80,64},{96,80},{112,96},{1... | collective-permute-start | bytes 1978376 | tf_op jit(solution)/shard_map/ppermute | solution.py:52
  154.7 16.7 %collective-permute-start.8 = (bf16[160,896]{1,0:T(8,128)(2,1)S(1)}, bf16[160,896]{1,0:T(8,128)(2,1)S(1)}, u32[]{:S(2)}, u32[]{:S(2)}) collective-permute-start(bf16[160,896]{1,0:T(8,128)(2,1)S(1)} %slice.171), channel_id=1, source_target_pairs={{0,16},{16,32},{32,48},{48,64},{64,80},{80,96},{96,112},{112,0},{1... | collective-permute-start | bytes 860168 | tf_op jit(solution)/shard_map/ppermute | solution.py:54
  161.5 15.5 %collective-permute-start.9 = (bf16[160,896]{1,0:T(8,128)(2,1)}, bf16[160,896]{1,0:T(8,128)(2,1)S(1)}, u32[]{:S(2)}, u32[]{:S(2)}) collective-permute-start(bf16[160,896]{1,0:T(8,128)(2,1)} %slice.172), channel_id=1, source_target_pairs={{0,112},{16,0},{32,16},{48,32},{64,48},{80,64},{96,80},{112,96},{1... | collective-permute-start | bytes 860168 | tf_op jit(solution)/shard_map/ppermute | solution.py:54
  185.5 33.7 %collective-permute-start.10 = (bf16[256,896]{1,0:T(8,128)(2,1)}, bf16[256,896]{1,0:T(8,128)(2,1)}, u32[]{:S(2)}, u32[]{:S(2)}) collective-permute-start(bf16[256,896]{1,0:T(8,128)(2,1)} %slice.242), channel_id=1, source_target_pairs={{0,128},{128,0},{1,129},{129,1},{2,130},{130,2},{3,131},{131,3},{4... | collective-permute-start | bytes 1376264 | tf_op jit(solution)/shard_map/ppermute | solution.py:194
  189.9 12.1 %collective-permute-start.18 = (bf16[184,896]{1,0:T(8,128)(2,1)}, bf16[184,896]{1,0:T(8,128)(2,1)}, u32[]{:S(2)}, u32[]{:S(2)}) collective-permute-start(bf16[184,896]{1,0:T(8,128)(2,1)} %slice.187), channel_id=1, source_target_pairs={{0,16},{16,32},{32,48},{48,64},{64,80},{80,96},{96,112},{112,0},{1... | collective-permute-start | bytes 989192 | tf_op jit(solution)/shard_map/ppermute | solution.py:54
  211.7 10.7 %collective-permute-start.19 = (bf16[256,896]{1,0:T(8,128)(2,1)}, bf16[256,896]{1,0:T(8,128)(2,1)}, u32[]{:S(2)}, u32[]{:S(2)}) collective-permute-start(bf16[256,896]{1,0:T(8,128)(2,1)} %slice.241), channel_id=1, source_target_pairs={{0,128},{128,0},{1,129},{129,1},{2,130},{130,2},{3,131},{131,3},{4... | collective-permute-start | bytes 1376264 | tf_op jit(solution)/shard_map/ppermute | solution.py:194
  243.6 11.1 %collective-permute-start.25 = (bf16[2,320,512]{2,1,0:T(8,128)(2,1)S(1)}, bf16[2,320,512]{2,1,0:T(8,128)(2,1)S(1)}, u32[]{:S(2)}, u32[]{:S(2)}) collective-permute-start(bf16[2,320,512]{2,1,0:T(8,128)(2,1)S(1)} %slice_bitcast_fusion), channel_id=1, source_target_pairs={{0,1},{1,0},{2,3},{3,2},{4,5},{5,4},{6,7},{7,6},{8,9},{9,8},{10,11... | collective-permute-start | bytes 1966088 | tf_op jit(solution)/shard_map/ppermute | solution.py:231
  258.1 11.8 %collective-permute-start.28 = (bf16[320,256]{1,0:T(8,128)(2,1)S(1)}, bf16[320,256]{1,0:T(8,128)(2,1)S(1)}, u32[]{:S(2)}, u32[]{:S(2)}) collective-permute-start(bf16[320,256]{1,0:T(8,128)(2,1)S(1)} %get-tuple-element.23), channel_id=1, source_target_pairs={{0,12},{4,0},{8,4},{12,8},{1,13},{5,1},{9,5},{13,9},{2,14},{6,2},{... | collective-permute-start | bytes 491528 | tf_op jit(solution)/shard_map/ppermute | solution.py:239
  258.5 11.6 %collective-permute-start.22 = (bf16[320,256]{1,0:T(8,128)(2,1)S(1)}, bf16[320,256]{1,0:T(8,128)(2,1)S(1)}, u32[]{:S(2)}, u32[]{:S(2)}) collective-permute-start(bf16[320,256]{1,0:T(8,128)(2,1)S(1)} %get-tuple-element.25), channel_id=1, source_target_pairs={{0,4},{4,8},{8,12},{12,0},{1,5},{5,9},{9,13},{13,1},{2,6},{6,10},{... | collective-permute-start | bytes 491528 | tf_op jit(solution)/shard_map/ppermute | solution.py:239
  262.2 11.4 %collective-permute-start.24 = (bf16[320,256]{1,0:T(8,128)(2,1)S(1)}, bf16[320,256]{1,0:T(8,128)(2,1)S(1)}, u32[]{:S(2)}, u32[]{:S(2)}) collective-permute-start(bf16[320,256]{1,0:T(8,128)(2,1)S(1)} %get-tuple-element.26), channel_id=1, source_target_pairs={{0,12},{4,0},{8,4},{12,8},{1,13},{5,1},{9,5},{13,9},{2,14},{6,2},{... | collective-permute-start | bytes 491528 | tf_op jit(solution)/shard_map/ppermute | solution.py:239
  274.0 12.1 %collective-permute-start.29 = (bf16[320,256]{1,0:T(8,128)(2,1)S(1)}, bf16[320,256]{1,0:T(8,128)(2,1)S(1)}, u32[]{:S(2)}, u32[]{:S(2)}) collective-permute-start(bf16[320,256]{1,0:T(8,128)(2,1)S(1)} %get-tuple-element.30), channel_id=1, source_target_pairs={{0,0},{2,2},{4,4},{6,6},{8,128},{10,130},{12,132},{14,134},{128,8}... | collective-permute-start | bytes 491528 | tf_op jit(solution)/shard_map/ppermute | solution.py:253
  (24 other events, 209.0 us)
Sparse Core Ops, SparseCore 0:
  42.8 99.5 all-gather.1
where the time goes:
time: 298 us; the launch traced here: 297 us
  waiting for transfers between devices  141 us (47%)
  starting transfers between devices  49 us (16%)
  Pallas kernels  37 us (12%)
  local copies, waits for them, and re-layouts  34 us (11%)
  between operations  17 us (6%)
  other arithmetic  11.7 us (4%)
  matrix products  7.94 us (3%)
    ppermute x6, waiting for transfers between devices, ring(): back = lax.ppermute(back, 'z', DOWN)  73.8 us
    ppermute x6, waiting for transfers between devices, ring(): fore = lax.ppermute(fore, 'z', UP)  36.1 us
    pallas_call x4, Pallas kernels, base_sum(): pl.pallas_call(functools.partial(base_kernel, count, depth), grid_spec=pl...  25.2 us
    pallas_call x2, Pallas kernels, part_products(): pl.pallas_call(part_kernel, grid_spec=pltpu.PrefetchScalarGridSpec(num_sc...  11.7 us
    ppermute x6, starting transfers between devices, body(): lax.ppermute(piece_for(x + d & NX - 1), 'x', [(i, (i + d) % NX) for i in...  10.1 us
    unnamed x41, local copies, waits for them, and re-layouts  8.95 us
    ppermute x2, starting transfers between devices, place(): lax.ppermute(at(quad, yl ^ flip), ('yh', 'x', 'yl'), perm).astype(F32)  8.57 us
    ppermute x6, starting transfers between devices, ring(): back = lax.ppermute(back, 'z', DOWN)  8.33 us
  transfers between devices with their start and end apart: 32, of which 18 were waited for; matrix products, arithmetic and copies ran while one was open for 17% of the time, Pallas kernels for 10%

commit v1 on v0

--- a/solution.py
+++ b/solution.py
@@ -176,7 +176,7 @@
 
     gates = ring(gate_weight)
     ups = ring(up_block)
-    downs = lax.all_gather(behind(down_weight, gates[2]), "z", axis=0, tiled=True)
+    downs = lax.all_gather(down_weight, "z", axis=0, tiled=True)
 
     where = jnp.stack([z, c])
     near = window(tokens, yh * half, half, 1)

time: 298 us -> 273 us (0.916)
  waiting for transfers between devices: 141 us -> 104 us
  starting transfers between devices: 49 us -> 61.1 us
    ppermute x6, waiting for transfers between devices: 73.8 us -> 8.68 us  [ring(): back = lax.ppermute(back, 'z', DOWN)]
    ppermute x6, waiting for transfers between devices: 36.1 us -> 63.5 us  [ring(): fore = lax.ppermute(fore, 'z', UP)]
    ppermute x6, starting transfers between devices: 8.33 us -> 21.6 us  [ring(): back = lax.ppermute(back, 'z', DOWN)]
    ppermute x2, waiting for transfers between devices: 5.68 us -> 0.01 us  [ring(): lax.ppermute(back[half:], 'z', DOWN)]
    ppermute x2, waiting for transfers between devices: 0.01 us -> 4.63 us  [ring(): lax.ppermute(fore[:half], 'z', UP)]
    ppermute x2, starting transfers between devices: 2.92 us -> 6.25 us  [ring(): lax.ppermute(back[half:], 'z', DOWN)]
    unnamed x41 -> x39, local copies, waits for them, and re-layouts: 8.95 us -> 8.17 us
  transfers between devices with their start and end apart: 32 -> 32, of which waited for: 18 -> 17; matrix products, arithmetic and copies ran while one was open for 17% -> 19% of each run, Pallas kernels for 10% -> 11%
where the time goes in v1:
time: 273 us; the launch traced here: 272 us
  waiting for transfers between devices  104 us (38%)
  starting transfers between devices  61.1 us (22%)
  Pallas kernels  37 us (14%)
  local copies, waits for them, and re-layouts  33.3 us (12%)
  between operations  17 us (6%)
  other arithmetic  11.7 us (4%)
  matrix products  7.94 us (3%)
    ppermute x6, waiting for transfers between devices, ring(): fore = lax.ppermute(fore, 'z', UP)  63.5 us
    pallas_call x4, Pallas kernels, base_sum(): pl.pallas_call(functools.partial(base_kernel, count, depth), grid_spec=pl...  25.3 us
    ppermute x6, starting transfers between devices, ring(): back = lax.ppermute(back, 'z', DOWN)  21.6 us
    pallas_call x2, Pallas kernels, part_products(): pl.pallas_call(part_kernel, grid_spec=pltpu.PrefetchScalarGridSpec(num_sc...  11.7 us
    ppermute x6, starting transfers between devices, body(): lax.ppermute(piece_for(x + d & NX - 1), 'x', [(i, (i + d) % NX) for i in...  10.1 us
    ppermute x6, waiting for transfers between devices, ring(): back = lax.ppermute(back, 'z', DOWN)  8.68 us
    ppermute x2, starting transfers between devices, place(): lax.ppermute(at(quad, yl ^ flip), ('yh', 'x', 'yl'), perm).astype(F32)  8.26 us
    unnamed x39, local copies, waits for them, and re-layouts  8.17 us
  transfers between devices with their start and end apart: 32, of which 17 were waited for; matrix products, arithmetic and copies ran while one was open for 19% of the time, Pallas kernels for 11%

profile of v1, /device:TPU:6, one launch (start us, length us, event | category | flops | bytes accessed | tf_op | source)
XLA Modules:
  0.0 271.8 jit_solution(8741489125582409698)
XLA Ops:
  9.7 3.3 %collective-permute-start = (bf16[24,896]{1,0:T(8,128)(2,1)S(1)}, bf16[24,896]{1,0:T(8,128)(2,1)S(1)}, u32[]{:S(2)}, u32[]{:S(2)}) collective-permute-start(bf16[24,896]{1,0:T(8,128)(2,1)S(1)} %concatenate.45), channel_id=1, source_target_pairs={{0,128},{128,0},{1,129},{129,1},{2,130},{130,2},{3,131},{131,3},{4... | collective-permute-start | bytes 129032 | tf_op jit(solution)/shard_map/ppermute | solution.py:174
  14.9 3.9 %collective-permute-start.5 = (bf16[320,896]{1,0:T(8,128)(2,1)}, bf16[320,896]{1,0:T(8,128)(2,1)}, u32[]{:S(2)}, u32[]{:S(2)}) collective-permute-start(bf16[320,896]{1,0:T(8,128)(2,1)} %refs_5_.1), channel_id=1, source_target_pairs={{0,112},{16,0},{32,16},{48,32},{64,48},{80,64},{96,80},{112,96},{1... | collective-permute-start | bytes 1720328 | tf_op jit(solution)/shard_map/ppermute | solution.py:52
  29.2 9.0 %collective-permute-done.2.refs_6_ = bf16[320,896]{1,0:T(8,128)(2,1)} collective-permute-done((bf16[320,896]{1,0:T(8,128)(2,1)}, bf16[320,896]{1,0:T(8,128)(2,1)}, u32[]{:S(2)}, u32[]{:S(2)}) %collective-permute-start.2) | collective-permute-done | bytes 573472 | tf_op jit(solution)/shard_map/ppermute | solution.py:51
  41.1 3.7 %collective-permute-start.6 = (bf16[320,896]{1,0:T(8,128)(2,1)}, bf16[320,896]{1,0:T(8,128)(2,1)}, u32[]{:S(2)}, u32[]{:S(2)}) collective-permute-start(bf16[320,896]{1,0:T(8,128)(2,1)} %collective-permute-done.5.refs_7_), channel_id=1, source_target_pairs={{0,112},{16,0},{32,16},{48,32},{64,48},{80,64},{96,80},{112,96},{1... | collective-permute-start | bytes 1720328 | tf_op jit(solution)/shard_map/ppermute | solution.py:52
  49.5 16.9 %collective-permute-done.11.refs_6_ = bf16[368,896]{1,0:T(8,128)(2,1)} collective-permute-done((bf16[368,896]{1,0:T(8,128)(2,1)S(1)}, bf16[368,896]{1,0:T(8,128)(2,1)}, u32[]{:S(2)}, u32[]{:S(2)}) %collective-permute-start.11) | collective-permute-done | bytes 659488 | tf_op jit(solution)/shard_map/ppermute | solution.py:51
  69.3 3.8 %collective-permute-start.15 = (bf16[368,896]{1,0:T(8,128)(2,1)}, bf16[368,896]{1,0:T(8,128)(2,1)}, u32[]{:S(2)}, u32[]{:S(2)}) collective-permute-start(bf16[368,896]{1,0:T(8,128)(2,1)} %collective-permute-done.14.refs_7_), channel_id=1, source_target_pairs={{0,112},{16,0},{32,16},{48,32},{64,48},{80,64},{96,80},{112,96},{1... | collective-permute-start | bytes 1978376 | tf_op jit(solution)/shard_map/ppermute | solution.py:52
  75.0 16.0 %collective-permute-done.3.refs_8_ = bf16[320,896]{1,0:T(8,128)(2,1)} collective-permute-done((bf16[320,896]{1,0:T(8,128)(2,1)}, bf16[320,896]{1,0:T(8,128)(2,1)}, u32[]{:S(2)}, u32[]{:S(2)}) %collective-permute-start.3) | collective-permute-done | bytes 573472 | tf_op jit(solution)/shard_map/ppermute | solution.py:51
  94.0 3.7 %collective-permute-start.7 = (bf16[320,896]{1,0:T(8,128)(2,1)}, bf16[320,896]{1,0:T(8,128)(2,1)}, u32[]{:S(2)}, u32[]{:S(2)}) collective-permute-start(bf16[320,896]{1,0:T(8,128)(2,1)} %collective-permute-done.6.refs_9_), channel_id=1, source_target_pairs={{0,112},{16,0},{32,16},{48,32},{64,48},{80,64},{96,80},{112,96},{1... | collective-permute-start | bytes 1720328 | tf_op jit(solution)/shard_map/ppermute | solution.py:52
  99.2 17.4 %collective-permute-done.12.refs_8_ = bf16[368,896]{1,0:T(8,128)(2,1)} collective-permute-done((bf16[368,896]{1,0:T(8,128)(2,1)}, bf16[368,896]{1,0:T(8,128)(2,1)}, u32[]{:S(2)}, u32[]{:S(2)}) %collective-permute-start.12) | collective-permute-done | bytes 659488 | tf_op jit(solution)/shard_map/ppermute | solution.py:51
  116.6 3.3 %collective-permute-start.16 = (bf16[368,896]{1,0:T(8,128)(2,1)}, bf16[368,896]{1,0:T(8,128)(2,1)}, u32[]{:S(2)}, u32[]{:S(2)}) collective-permute-start(bf16[368,896]{1,0:T(8,128)(2,1)} %collective-permute-done.15.refs_9_), channel_id=1, source_target_pairs={{0,112},{16,0},{32,16},{48,32},{64,48},{80,64},{96,80},{112,96},{1... | collective-permute-start | bytes 1978376 | tf_op jit(solution)/shard_map/ppermute | solution.py:52
  124.6 4.3 %collective-permute-done.4.refs_3_ = bf16[320,896]{1,0:T(8,128)(2,1)} collective-permute-done((bf16[320,896]{1,0:T(8,128)(2,1)}, bf16[320,896]{1,0:T(8,128)(2,1)}, u32[]{:S(2)}, u32[]{:S(2)}) %collective-permute-start.4) | collective-permute-done | bytes 573472 | tf_op jit(solution)/shard_map/ppermute | solution.py:51
  136.4 6.9 %shard_map.174.refs_6_ = f32[512,896]{1,0:T(8,128)} custom-call(s32[2]{0:T(128)} %pad_add_fusion.where, bf16[8,512,320]{2,1,0:T(8,128)(2,1)} %bitcast.130, bf16[8,512,320]{2,1,0:T(8,128)(2,1)} %bitcast.131, bf16[8,512,320]{2,1,0:T(8,128)(2,1)} %bitcast.132, bf16[8,512,320]{2,1,0:T(8,128)(2,1)} %bitcast.133, bf16[8,512,320]{2,1,0:T(8,128)(2,1)} %bitcast.134, ...), custom_call_target="tpu_custom_call" | custom-call | flops 1468006400 | bytes 6340608 | tf_op jit(solution)/shard_map/pallas_call | solution.py:79
  143.3 4.6 %collective-permute-done.8 = bf16[160,896]{1,0:T(8,128)(2,1)S(1)} collective-permute-done((bf16[160,896]{1,0:T(8,128)(2,1)S(1)}, bf16[160,896]{1,0:T(8,128)(2,1)S(1)}, u32[]{:S(2)}, u32[]{:S(2)}) %collective-permute-start.8) | collective-permute-done | bytes 286752 | tf_op jit(solution)/shard_map/ppermute | solution.py:54
  148.7 5.6 %shard_map.175 = f32[512,896]{1,0:T(8,128)} custom-call(s32[2]{0:T(128)} %pad_add_fusion.where, bf16[8,512,320]{2,1,0:T(8,128)(2,1)} %bitcast.135, bf16[8,512,320]{2,1,0:T(8,128)(2,1)} %bitcast.136, bf16[8,512,320]{2,1,0:T(8,128)(2,1)} %bitcast.137, bf16[320,896]{1,0:T(8,128)(2,1)} %collective-permute-done.4.refs_3_, ...), custom_call_target="tpu_custom_call" | custom-call | flops 880803840 | bytes 4538368 | tf_op jit(solution)/shard_map/pallas_call | solution.py:79
  162.3 7.2 %shard_map.176.refs_6_ = f32[512,896]{1,0:T(8,128)} custom-call(s32[2]{0:T(128)} %pad_add_fusion.where, bf16[8,512,320]{2,1,0:T(8,128)(2,1)} %bitcast.138, bf16[8,512,320]{2,1,0:T(8,128)(2,1)} %bitcast.139, bf16[8,512,320]{2,1,0:T(8,128)(2,1)} %bitcast.140, bf16[8,512,320]{2,1,0:T(8,128)(2,1)} %bitcast.141, bf16[8,512,320]{2,1,0:T(8,128)(2,1)} %bitcast.142, ...), custom_call_target="tpu_custom_call" | custom-call | flops 1468006400 | bytes 6340608 | tf_op jit(solution)/shard_map/pallas_call | solution.py:79
  176.0 5.7 %shard_map.177 = f32[512,896]{1,0:T(8,128)} custom-call(s32[2]{0:T(128)} %pad_add_fusion.where, bf16[8,512,320]{2,1,0:T(8,128)(2,1)} %bitcast.143, bf16[8,512,320]{2,1,0:T(8,128)(2,1)} %bitcast.144, bf16[8,512,320]{2,1,0:T(8,128)(2,1)} %bitcast.145, bf16[368,896]{1,0:T(8,128)(2,1)} %copy-done.4, bf16[368,896]{1,0:T(8,128)(2,1)} %collective-permute-done.16.refs_4_, ...), custom_call_target="tpu_custom_call" | custom-call | flops 880803840 | bytes 4538368 | tf_op jit(solution)/shard_map/pallas_call | solution.py:79
  191.1 4.9 %collective-permute-done.19 = bf16[256,896]{1,0:T(8,128)(2,1)} collective-permute-done((bf16[256,896]{1,0:T(8,128)(2,1)}, bf16[256,896]{1,0:T(8,128)(2,1)}, u32[]{:S(2)}, u32[]{:S(2)}) %collective-permute-start.19) | collective-permute-done | bytes 458784 | tf_op jit(solution)/shard_map/ppermute | solution.py:194
  201.6 7.9 %collective-permute-done.20 = bf16[256,896]{1,0:T(8,128)(2,1)S(1)} collective-permute-done((bf16[256,896]{1,0:T(8,128)(2,1)S(1)}, bf16[256,896]{1,0:T(8,128)(2,1)S(1)}, u32[]{:S(2)}, u32[]{:S(2)}) %collective-permute-start.20) | collective-permute-done | bytes 458784 | tf_op jit(solution)/shard_map/ppermute | solution.py:218
  211.4 5.9 %shard_map.179 = bf16[2,2,320,512]{3,2,1,0:T(8,128)(2,1)} custom-call(s32[2]{0:T(128)} %pad_add_fusion.where, bf16[512,896]{1,0:T(8,128)(2,1)} %pad_maximum_fusion.1.hidden, f32[1,512]{1,0:T(1,128)} %maximum_multiply_fusion.across, f32[8,320,2]{2,1,0:T(8,128)} %bitcast.146, bf16[2560,896]{1,0:T(8,128)(2,1)} %all-gather.2.cloned.1.call-done.block), custom_call_target="tpu_custom_call" | custom-call | flops 1174405120 | bytes 4521984 | tf_op jit(solution)/shard_map/pallas_call | solution.py:117
  220.4 5.8 %shard_map.178 = bf16[2,2,320,512]{3,2,1,0:T(8,128)(2,1)} custom-call(s32[2]{0:T(128)} %pad_add_fusion.where, bf16[512,896]{1,0:T(8,128)(2,1)} %pad_maximum_fusion.1.hidden, f32[1,512]{1,0:T(1,128)} %maximum_multiply_fusion.across, f32[8,320,2]{2,1,0:T(8,128)} %bitcast.147, bf16[2560,896]{1,0:T(8,128)(2,1)} %all-gather.2.cloned.1.call-done.block), custom_call_target="tpu_custom_call" | custom-call | flops 1174405120 | bytes 4521984 | tf_op jit(solution)/shard_map/pallas_call | solution.py:117
  233.4 3.3 %collective-permute-start.22 = (bf16[320,256]{1,0:T(8,128)(2,1)S(1)}, bf16[320,256]{1,0:T(8,128)(2,1)S(1)}, u32[]{:S(2)}, u32[]{:S(2)}) collective-permute-start(bf16[320,256]{1,0:T(8,128)(2,1)S(1)} %get-tuple-element.23), channel_id=1, source_target_pairs={{0,4},{4,8},{8,12},{12,0},{1,5},{5,9},{9,13},{13,1},{2,6},{6,10},{... | collective-permute-start | bytes 491528 | tf_op jit(solution)/shard_map/ppermute | solution.py:239
  237.1 3.7 %collective-permute-start.24 = (bf16[320,256]{1,0:T(8,128)(2,1)S(1)}, bf16[320,256]{1,0:T(8,128)(2,1)S(1)}, u32[]{:S(2)}, u32[]{:S(2)}) collective-permute-start(bf16[320,256]{1,0:T(8,128)(2,1)S(1)} %get-tuple-element.24), channel_id=1, source_target_pairs={{0,12},{4,0},{8,4},{12,8},{1,13},{5,1},{9,5},{13,9},{2,14},{6,2},{... | collective-permute-start | bytes 491528 | tf_op jit(solution)/shard_map/ppermute | solution.py:239
  240.8 4.0 %collective-permute-done.28 = bf16[320,256]{1,0:T(8,128)(2,1)S(1)} collective-permute-done((bf16[320,256]{1,0:T(8,128)(2,1)S(1)}, bf16[320,256]{1,0:T(8,128)(2,1)S(1)}, u32[]{:S(2)}, u32[]{:S(2)}) %collective-permute-start.28) | collective-permute-done | bytes 163872 | tf_op jit(solution)/shard_map/ppermute | solution.py:239
  248.9 5.9 %collective-permute-start.29 = (bf16[320,256]{1,0:T(8,128)(2,1)S(1)}, bf16[320,256]{1,0:T(8,128)(2,1)S(1)}, u32[]{:S(2)}, u32[]{:S(2)}) collective-permute-start(bf16[320,256]{1,0:T(8,128)(2,1)S(1)} %get-tuple-element.28), channel_id=1, source_target_pairs={{0,0},{2,2},{4,4},{6,6},{8,128},{10,130},{12,132},{14,134},{128,8}... | collective-permute-start | bytes 491528 | tf_op jit(solution)/shard_map/ppermute | solution.py:253
  (141 shorter events, 98.2 us)
Async XLA Ops:
  7.2 204.2 %all-gather.2.cloned.1.call-start = ((), (), s32[]{:S(2)}) async-start(), calls=%async_computation | async-start | bytes 5160960 | tf_op jit(solution)/shard_map/all_gather | solution.py:179
  13.0 25.2 %collective-permute-start.2 = (bf16[320,896]{1,0:T(8,128)(2,1)}, bf16[320,896]{1,0:T(8,128)(2,1)}, u32[]{:S(2)}, u32[]{:S(2)}) collective-permute-start(bf16[320,896]{1,0:T(8,128)(2,1)} %refs_5_.1), channel_id=1, source_target_pairs={{0,16},{16,32},{32,48},{48,64},{64,80},{80,96},{96,112},{112,0},{1... | collective-permute-start | bytes 1720328 | tf_op jit(solution)/shard_map/ppermute | solution.py:51
  14.9 26.2 %collective-permute-start.5 = (bf16[320,896]{1,0:T(8,128)(2,1)}, bf16[320,896]{1,0:T(8,128)(2,1)}, u32[]{:S(2)}, u32[]{:S(2)}) collective-permute-start(bf16[320,896]{1,0:T(8,128)(2,1)} %refs_5_.1), channel_id=1, source_target_pairs={{0,112},{16,0},{32,16},{48,32},{64,48},{80,64},{96,80},{112,96},{1... | collective-permute-start | bytes 1720328 | tf_op jit(solution)/shard_map/ppermute | solution.py:52
  19.9 46.6 %collective-permute-start.11 = (bf16[368,896]{1,0:T(8,128)(2,1)S(1)}, bf16[368,896]{1,0:T(8,128)(2,1)}, u32[]{:S(2)}, u32[]{:S(2)}) collective-permute-start(bf16[368,896]{1,0:T(8,128)(2,1)S(1)} %concatenate.49.refs_5_), channel_id=1, source_target_pairs={{0,16},{16,32},{32,48},{48,64},{64,80},{80,96},{96,112},{112,0},{1... | collective-permute-start | bytes 1978376 | tf_op jit(solution)/shard_map/ppermute | solution.py:51
  20.0 49.3 %collective-permute-start.14 = (bf16[368,896]{1,0:T(8,128)(2,1)S(1)}, bf16[368,896]{1,0:T(8,128)(2,1)}, u32[]{:S(2)}, u32[]{:S(2)}) collective-permute-start(bf16[368,896]{1,0:T(8,128)(2,1)S(1)} %concatenate.49.refs_5_), channel_id=1, source_target_pairs={{0,112},{16,0},{32,16},{48,32},{64,48},{80,64},{96,80},{112,96},{1... | collective-permute-start | bytes 1978376 | tf_op jit(solution)/shard_map/ppermute | solution.py:52
  26.9 92.9 %collective-permute-start.1 = (bf16[256,2560]{0,1:T(8,128)(2,1)}, bf16[256,2560]{0,1:T(8,128)(2,1)}, u32[]{:S(2)}, u32[]{:S(2)}) collective-permute-start(bf16[256,2560]{0,1:T(8,128)(2,1)} %copy.30), channel_id=1, source_target_pairs={{0,128},{128,0},{1,129},{129,1},{2,130},{130,2},{3,131},{131,3},{4... | collective-permute-start | bytes 3932168 | tf_op jit(solution)/shard_map/ppermute | solution.py:184
  38.2 52.8 %collective-permute-start.3 = (bf16[320,896]{1,0:T(8,128)(2,1)}, bf16[320,896]{1,0:T(8,128)(2,1)}, u32[]{:S(2)}, u32[]{:S(2)}) collective-permute-start(bf16[320,896]{1,0:T(8,128)(2,1)} %collective-permute-done.2.refs_6_), channel_id=1, source_target_pairs={{0,16},{16,32},{32,48},{48,64},{64,80},{80,96},{96,112},{112,0},{1... | collective-permute-start | bytes 1720328 | tf_op jit(solution)/shard_map/ppermute | solution.py:51
  41.1 52.8 %collective-permute-start.6 = (bf16[320,896]{1,0:T(8,128)(2,1)}, bf16[320,896]{1,0:T(8,128)(2,1)}, u32[]{:S(2)}, u32[]{:S(2)}) collective-permute-start(bf16[320,896]{1,0:T(8,128)(2,1)} %collective-permute-done.5.refs_7_), channel_id=1, source_target_pairs={{0,112},{16,0},{32,16},{48,32},{64,48},{80,64},{96,80},{112,96},{1... | collective-permute-start | bytes 1720328 | tf_op jit(solution)/shard_map/ppermute | solution.py:52
  66.5 50.1 %collective-permute-start.12 = (bf16[368,896]{1,0:T(8,128)(2,1)}, bf16[368,896]{1,0:T(8,128)(2,1)}, u32[]{:S(2)}, u32[]{:S(2)}) collective-permute-start(bf16[368,896]{1,0:T(8,128)(2,1)} %collective-permute-done.11.refs_6_), channel_id=1, source_target_pairs={{0,16},{16,32},{32,48},{48,64},{64,80},{80,96},{96,112},{112,0},{1... | collective-permute-start | bytes 1978376 | tf_op jit(solution)/shard_map/ppermute | solution.py:51
  69.3 47.3 %collective-permute-start.15 = (bf16[368,896]{1,0:T(8,128)(2,1)}, bf16[368,896]{1,0:T(8,128)(2,1)}, u32[]{:S(2)}, u32[]{:S(2)}) collective-permute-start(bf16[368,896]{1,0:T(8,128)(2,1)} %collective-permute-done.14.refs_7_), channel_id=1, source_target_pairs={{0,112},{16,0},{32,16},{48,32},{64,48},{80,64},{96,80},{112,96},{1... | collective-permute-start | bytes 1978376 | tf_op jit(solution)/shard_map/ppermute | solution.py:52
  91.0 37.8 %collective-permute-start.4 = (bf16[320,896]{1,0:T(8,128)(2,1)}, bf16[320,896]{1,0:T(8,128)(2,1)}, u32[]{:S(2)}, u32[]{:S(2)}) collective-permute-start(bf16[320,896]{1,0:T(8,128)(2,1)} %collective-permute-done.3.refs_8_), channel_id=1, source_target_pairs={{0,16},{16,32},{32,48},{48,64},{64,80},{80,96},{96,112},{112,0},{1... | collective-permute-start | bytes 1720328 | tf_op jit(solution)/shard_map/ppermute | solution.py:51
  94.0 36.0 %collective-permute-start.7 = (bf16[320,896]{1,0:T(8,128)(2,1)}, bf16[320,896]{1,0:T(8,128)(2,1)}, u32[]{:S(2)}, u32[]{:S(2)}) collective-permute-start(bf16[320,896]{1,0:T(8,128)(2,1)} %collective-permute-done.6.refs_9_), channel_id=1, source_target_pairs={{0,112},{16,0},{32,16},{48,32},{64,48},{80,64},{96,80},{112,96},{1... | collective-permute-start | bytes 1720328 | tf_op jit(solution)/shard_map/ppermute | solution.py:52
  116.6 44.9 %collective-permute-start.13 = (bf16[368,896]{1,0:T(8,128)(2,1)}, bf16[368,896]{1,0:T(8,128)(2,1)S(1)}, u32[]{:S(2)}, u32[]{:S(2)}) collective-permute-start(bf16[368,896]{1,0:T(8,128)(2,1)} %collective-permute-done.12.refs_8_), channel_id=1, source_target_pairs={{0,16},{16,32},{32,48},{48,64},{64,80},{80,96},{96,112},{112,0},{1... | collective-permute-start | bytes 1978376 | tf_op jit(solution)/shard_map/ppermute | solution.py:51
  116.6 40.2 %collective-permute-start.16 = (bf16[368,896]{1,0:T(8,128)(2,1)}, bf16[368,896]{1,0:T(8,128)(2,1)}, u32[]{:S(2)}, u32[]{:S(2)}) collective-permute-start(bf16[368,896]{1,0:T(8,128)(2,1)} %collective-permute-done.15.refs_9_), channel_id=1, source_target_pairs={{0,112},{16,0},{32,16},{48,32},{64,48},{80,64},{96,80},{112,96},{1... | collective-permute-start | bytes 1978376 | tf_op jit(solution)/shard_map/ppermute | solution.py:52
  129.8 18.0 %collective-permute-start.8 = (bf16[160,896]{1,0:T(8,128)(2,1)S(1)}, bf16[160,896]{1,0:T(8,128)(2,1)S(1)}, u32[]{:S(2)}, u32[]{:S(2)}) collective-permute-start(bf16[160,896]{1,0:T(8,128)(2,1)S(1)} %slice.171), channel_id=1, source_target_pairs={{0,16},{16,32},{32,48},{48,64},{64,80},{80,96},{96,112},{112,0},{1... | collective-permute-start | bytes 860168 | tf_op jit(solution)/shard_map/ppermute | solution.py:54
  131.6 16.2 %collective-permute-start.9 = (bf16[160,896]{1,0:T(8,128)(2,1)}, bf16[160,896]{1,0:T(8,128)(2,1)S(1)}, u32[]{:S(2)}, u32[]{:S(2)}) collective-permute-start(bf16[160,896]{1,0:T(8,128)(2,1)} %slice.172), channel_id=1, source_target_pairs={{0,112},{16,0},{32,16},{48,32},{64,48},{80,64},{96,80},{112,96},{1... | collective-permute-start | bytes 860168 | tf_op jit(solution)/shard_map/ppermute | solution.py:54
  156.4 34.8 %collective-permute-start.10 = (bf16[256,896]{1,0:T(8,128)(2,1)}, bf16[256,896]{1,0:T(8,128)(2,1)}, u32[]{:S(2)}, u32[]{:S(2)}) collective-permute-start(bf16[256,896]{1,0:T(8,128)(2,1)} %slice.242), channel_id=1, source_target_pairs={{0,128},{128,0},{1,129},{129,1},{2,130},{130,2},{3,131},{131,3},{4... | collective-permute-start | bytes 1376264 | tf_op jit(solution)/shard_map/ppermute | solution.py:194
  162.3 11.7 %collective-permute-start.18 = (bf16[184,896]{1,0:T(8,128)(2,1)}, bf16[184,896]{1,0:T(8,128)(2,1)}, u32[]{:S(2)}, u32[]{:S(2)}) collective-permute-start(bf16[184,896]{1,0:T(8,128)(2,1)} %slice.187), channel_id=1, source_target_pairs={{0,16},{16,32},{32,48},{48,64},{64,80},{80,96},{96,112},{112,0},{1... | collective-permute-start | bytes 989192 | tf_op jit(solution)/shard_map/ppermute | solution.py:54
  183.6 12.5 %collective-permute-start.19 = (bf16[256,896]{1,0:T(8,128)(2,1)}, bf16[256,896]{1,0:T(8,128)(2,1)}, u32[]{:S(2)}, u32[]{:S(2)}) collective-permute-start(bf16[256,896]{1,0:T(8,128)(2,1)} %slice.241), channel_id=1, source_target_pairs={{0,128},{128,0},{1,129},{129,1},{2,130},{130,2},{3,131},{131,3},{4... | collective-permute-start | bytes 1376264 | tf_op jit(solution)/shard_map/ppermute | solution.py:194
  198.0 11.5 %collective-permute-start.20 = (bf16[256,896]{1,0:T(8,128)(2,1)S(1)}, bf16[256,896]{1,0:T(8,128)(2,1)S(1)}, u32[]{:S(2)}, u32[]{:S(2)}) collective-permute-start(bf16[256,896]{1,0:T(8,128)(2,1)S(1)} %fusion.5), channel_id=1, source_target_pairs={{0,128},{128,0},{1,129},{129,1},{2,130},{130,2},{3,131},{131,3},{4... | collective-permute-start | bytes 1376264 | tf_op jit(solution)/shard_map/ppermute | solution.py:218
  233.0 11.9 %collective-permute-start.28 = (bf16[320,256]{1,0:T(8,128)(2,1)S(1)}, bf16[320,256]{1,0:T(8,128)(2,1)S(1)}, u32[]{:S(2)}, u32[]{:S(2)}) collective-permute-start(bf16[320,256]{1,0:T(8,128)(2,1)S(1)} %get-tuple-element.21), channel_id=1, source_target_pairs={{0,12},{4,0},{8,4},{12,8},{1,13},{5,1},{9,5},{13,9},{2,14},{6,2},{... | collective-permute-start | bytes 491528 | tf_op jit(solution)/shard_map/ppermute | solution.py:239
  233.4 11.6 %collective-permute-start.22 = (bf16[320,256]{1,0:T(8,128)(2,1)S(1)}, bf16[320,256]{1,0:T(8,128)(2,1)S(1)}, u32[]{:S(2)}, u32[]{:S(2)}) collective-permute-start(bf16[320,256]{1,0:T(8,128)(2,1)S(1)} %get-tuple-element.23), channel_id=1, source_target_pairs={{0,4},{4,8},{8,12},{12,0},{1,5},{5,9},{9,13},{13,1},{2,6},{6,10},{... | collective-permute-start | bytes 491528 | tf_op jit(solution)/shard_map/ppermute | solution.py:239
  237.1 11.4 %collective-permute-start.24 = (bf16[320,256]{1,0:T(8,128)(2,1)S(1)}, bf16[320,256]{1,0:T(8,128)(2,1)S(1)}, u32[]{:S(2)}, u32[]{:S(2)}) collective-permute-start(bf16[320,256]{1,0:T(8,128)(2,1)S(1)} %get-tuple-element.24), channel_id=1, source_target_pairs={{0,12},{4,0},{8,4},{12,8},{1,13},{5,1},{9,5},{13,9},{2,14},{6,2},{... | collective-permute-start | bytes 491528 | tf_op jit(solution)/shard_map/ppermute | solution.py:239
  248.9 12.4 %collective-permute-start.29 = (bf16[320,256]{1,0:T(8,128)(2,1)S(1)}, bf16[320,256]{1,0:T(8,128)(2,1)S(1)}, u32[]{:S(2)}, u32[]{:S(2)}) collective-permute-start(bf16[320,256]{1,0:T(8,128)(2,1)S(1)} %get-tuple-element.28), channel_id=1, source_target_pairs={{0,0},{2,2},{4,4},{6,6},{8,128},{10,130},{12,132},{14,134},{128,8}... | collective-permute-start | bytes 491528 | tf_op jit(solution)/shard_map/ppermute | solution.py:253
  (23 other events, 188.4 us)
Sparse Core Ops, SparseCore 0:
  9.8 104.5 all-gather.1
